TPU v7x, 256 devices: a whole 4x4x8 slice. The times are simulated.
256 devices in a mesh: ctx: 64 (over x, z, core), head: 4 (over y).
Axes of the slice: x: 4, y: 4, z: 8, core: 2. Of those that a mesh axis runs over, the one named last changes fastest.
Arguments:
- queries: bfloat16 [12288, 512], P('ctx', 'head'), may hold values from -32 to 32, as said below
- key_rows: bfloat16 [12288, 512], P('ctx', 'head'), may hold values from -12 to 12
- value_rows: bfloat16 [12288, 512], P('ctx', 'head'), may hold values from -5 to 5
- out_grads: bfloat16 [12288, 512], P('ctx', 'head'), may hold values from -5 to 5
- query_proj: bfloat16 [5120, 512], P(None, 'head'), may hold values from -0.25 to 0.25
- key_proj: bfloat16 [5120, 512], P(None, 'head'), may hold values from -0.25 to 0.25
- value_proj: bfloat16 [5120, 512], P(None, 'head'), may hold values from -0.25 to 0.25
Outputs:
- d_input: bfloat16 [12288, 5120], P('ctx', 'head')
Inputs may be any that keep to these rules, and one draw needn't show every extreme that they name: queries of one head times its keys stay of order one on most rows; some rows may be much larger.
All inputs are finite; a program needn't handle non-finite values.
Results may differ from a plain program's by a relative error of at most 0.0063.
Values may be sent and summed in bfloat16 or wider, within the bound.
No kernel may reach another device: no remote copies, remote signals or barrier semaphores. Data moves between devices by JAX's collectives and lax.ppermute only.
A program may use at most 64 MiB of HBM per device.

v0:
```python
import functools
import math

import jax
import jax.numpy as jnp
from jax import lax
from jax.experimental import pallas as pl
from jax.experimental.pallas import tpu as pltpu
from jax.sharding import PartitionSpec as P

ROWS = 192
WIDTH = 128
QUARTER = 2 * ROWS
TILE = 8 * ROWS
SCALE = 1.0 / math.sqrt(WIDTH)
SCALE_LOG2 = SCALE / math.log(2.0)
LOWEST = -1e30
CONTRACT_LAST = (((1,), (1,)), ((), ()))
QUERY_SHIFTS = [(sx, se) for sx in range(4) for se in range(2)]
KEY_SHIFTS = [(st, sc) for sc in range(2) for st in (0, 2, 1, 3)]
STEPS = (2, 1, 3)


def place(x, t, e, c):
    return 16 * (x % 4) + 4 * (t % 4) + 2 * e + c


def pairs_of(move):
    return [
        (place(x, t, e, c), place(*move(x, t, e, c)))
        for x in range(4)
        for t in range(4)
        for e in range(2)
        for c in range(2)
    ]


def to_neighbour(value):
    return to_query_member(value, 0, 1)


def to_query_member(value, sx, se):
    return lax.ppermute(value, "ctx", pairs_of(lambda x, t, e, c: (x ^ sx, t, e ^ se, c)))


def to_key_member(value, st):
    return lax.ppermute(value, "ctx", pairs_of(lambda x, t, e, c: (x - t + (t ^ st), t ^ st, e, c)))


def to_other_core(value):
    return lax.ppermute(value, "ctx", pairs_of(lambda x, t, e, c: (x, t, e, 1 - c)))


QUERY_GROUPS = [
    [place(x, t, e, c) for x in range(4) for e in range(2)] for t in range(4) for c in range(2)
]


def exchange(value, groups):
    return lax.all_to_all(value, "ctx", 0, 0, axis_index_groups=groups, tiled=True)


def coordinates(ctx_index):
    return ctx_index // 16, (ctx_index // 4) % 4, (ctx_index // 2) % 2, ctx_index % 2


def slot_rows(slot):
    return pl.ds(pl.multiple_of(slot * ROWS, ROWS), ROWS)


def query_slot(ctx_index, sx, se):
    x, _, e, _ = coordinates(ctx_index)
    return (x ^ sx) * 2 + (e ^ se)


def key_slot(ctx_index, st, sc):
    x, t, _, c = coordinates(ctx_index)
    return ((x - t + (t ^ st) + 4) % 4) * 2 + (c ^ sc)


def diagonal_mask(ctx_index, quarter):
    x, t, e, c = coordinates(ctx_index)
    key_t = (quarter - x + t + 4) % 4
    key_first = (16 * quarter + 4 * key_t + 2 * e) * ROWS
    query_first = (16 * quarter + 4 * t + c) * ROWS
    keys = key_first + lax.broadcasted_iota(jnp.int32, (QUARTER, QUARTER), 0)
    columns = lax.broadcasted_iota(jnp.int32, (1, QUARTER), 1)
    queries = query_first + columns + jnp.where(columns >= ROWS, ROWS, 0)
    return queries >= keys


def chunk_scores(ctx_index, query_ref, key_ref, query_quarter, key_quarter):
    query_rows = pl.ds(query_quarter * QUARTER, QUARTER)
    key_rows = pl.ds(key_quarter * QUARTER, QUARTER)
    queries, out_grads = query_ref[query_rows, :WIDTH], query_ref[query_rows, WIDTH:]
    keys, values = key_ref[key_rows, :WIDTH], key_ref[key_rows, WIDTH:]
    scores = lax.dot_general(keys, queries, CONTRACT_LAST, preferred_element_type=jnp.float32)
    scores = scores * SCALE_LOG2
    if query_quarter == key_quarter:
        scores = jnp.where(diagonal_mask(ctx_index, query_quarter), scores, 2.0 * LOWEST)
    d_prob = lax.dot_general(values, out_grads, CONTRACT_LAST, preferred_element_type=jnp.float32)
    return queries, out_grads, scores, d_prob


def band_scores(ctx_index, query_ref, key_ref, quarter):
    key_rows = pl.ds(quarter * QUARTER, QUARTER)
    queries, out_grads = query_ref[quarter * QUARTER :, :WIDTH], query_ref[quarter * QUARTER :, WIDTH:]
    keys, values = key_ref[key_rows, :WIDTH], key_ref[key_rows, WIDTH:]
    scores = lax.dot_general(keys, queries, CONTRACT_LAST, preferred_element_type=jnp.float32)
    scores = scores * SCALE_LOG2
    first = jnp.where(diagonal_mask(ctx_index, quarter), scores[:, :QUARTER], 2.0 * LOWEST)
    scores = first if quarter == 3 else jnp.concatenate([first, scores[:, QUARTER:]], axis=1)
    d_prob = lax.dot_general(values, out_grads, CONTRACT_LAST, preferred_element_type=jnp.float32)
    return queries, out_grads, scores, d_prob


def stats_kernel(ctx_ref, *refs):
    query_refs, key_refs, (query_ref, key_ref, stats_ref) = refs[:8], refs[8:16], refs[16:]
    ctx_index = ctx_ref[0]
    for (sx, se), ref in zip(QUERY_SHIFTS, query_refs):
        query_ref[slot_rows(query_slot(ctx_index, sx, se)), :] = ref[...]
    for (st, sc), ref in zip(KEY_SHIFTS, key_refs):
        key_ref[slot_rows(key_slot(ctx_index, st, sc)), :] = ref[...]
    for query_quarter in range(4):
        run_max = jnp.full((1, QUARTER), LOWEST, jnp.float32)
        run_total = jnp.zeros((1, QUARTER), jnp.float32)
        run_dot = jnp.zeros((1, QUARTER), jnp.float32)
        for key_quarter in range(query_quarter + 1):
            _, _, scores, d_prob = chunk_scores(
                ctx_index, query_ref, key_ref, query_quarter, key_quarter
            )
            new_max = jnp.maximum(run_max, jnp.max(scores, axis=0, keepdims=True))
            weights = jnp.exp2(scores - new_max)
            fade = jnp.exp2(run_max - new_max)
            run_total = run_total * fade + jnp.sum(weights, axis=0, keepdims=True)
            run_dot = run_dot * fade + jnp.sum(weights * d_prob, axis=0, keepdims=True)
            run_max = new_max
        some = run_total > 0.0
        log_total = jnp.where(some, run_max + jnp.log2(jnp.where(some, run_total, 1.0)), LOWEST)
        grad_dot = run_dot / jnp.where(some, run_total, 1.0)
        for part in range(3):
            row, lanes = 3 * query_quarter + part, slice(part * WIDTH, (part + 1) * WIDTH)
            for copy in range(0, 8 * 24, 24):
                stats_ref[copy + row : copy + row + 1, :] = log_total[:, lanes]
                stats_ref[copy + 12 + row : copy + 13 + row, :] = grad_dot[:, lanes]


def grads_kernel(ctx_ref, query_ref, key_ref, stats_ref, *refs):
    query_out, own_out, other_out, d_query_ref, d_pair_ref, turned_ref = refs[:4], *refs[4:]
    ctx_index = ctx_ref[0]
    totals = [stats_ref[24 * i : 24 * i + 12, :] for i in range(8)]
    dots = [stats_ref[24 * i + 12 : 24 * i + 24, :] for i in range(8)]
    top = functools.reduce(jnp.maximum, totals)
    shares = [jnp.exp2(total - top) for total in totals]
    share_sum = sum(shares)
    log_total = top + jnp.log2(share_sum)
    grad_dot = sum(share * dot for share, dot in zip(shares, dots)) / share_sum
    keys_turned = key_ref[:, :WIDTH].T
    row_log = jnp.concatenate([log_total[row : row + 1, :] for row in range(12)], axis=1)
    row_dot = jnp.concatenate([grad_dot[row : row + 1, :] for row in range(12)], axis=1)
    for quarter in range(4):
        first = quarter * QUARTER
        queries, out_grads, scores, d_prob = band_scores(ctx_index, query_ref, key_ref, quarter)
        weights = jnp.exp2(scores - row_log[:, first:])
        d_score = (weights * (d_prob - row_dot[:, first:]) * SCALE).astype(jnp.bfloat16)
        weights_low = weights.astype(jnp.bfloat16)
        key_rows = pl.ds(first, QUARTER)
        d_pair_ref[key_rows, :WIDTH] = jnp.dot(
            d_score, queries, preferred_element_type=jnp.float32
        )
        d_pair_ref[key_rows, WIDTH:] = jnp.dot(
            weights_low, out_grads, preferred_element_type=jnp.float32
        )
        turned = keys_turned[:, first : first + QUARTER]
        part = jnp.dot(turned, d_score, preferred_element_type=jnp.float32)
        if quarter == 0:
            turned_ref[...] = part
        else:
            turned_ref[:, first:] += part
    d_query_ref[...] = turned_ref[...].T
    for sx, se in QUERY_SHIFTS:
        slot = slot_rows(query_slot(ctx_index, sx, se))
        part_rows = slice(se * ROWS, (se + 1) * ROWS)
        query_out[sx][part_rows, :] = d_query_ref[slot, :].astype(query_out[sx].dtype)
    for st, sc in KEY_SHIFTS:
        slot = slot_rows(key_slot(ctx_index, st, sc))
        out = other_out if sc else own_out
        out[st * ROWS : (st + 1) * ROWS, :] = d_pair_ref[slot, :].astype(out.dtype)


def pack_kernel(core_ref, *refs):
    sources, targets = refs[:7], refs[7:10]
    buffers, (in_sems, out_sems) = refs[10:13], refs[13:]
    half = targets[2].shape[0] // 4
    lanes = [pl.ds(index * WIDTH, WIDTH) for index in range(3)]
    parts = list(zip(targets, buffers))[:2]
    into = [
        [(sources[3 + 2 * pair + index], buffers[pair].at[:, lanes[index]]) for index in range(2)]
        for pair in range(2)
    ]
    for owner in range(4):
        first = pl.multiple_of((2 * owner + core_ref[0]) * half, half)
        rows = pl.ds(owner * half, half)
        parts.append((targets[2].at[rows, :], buffers[2].at[rows, :]))
        into.append(
            [
                (sources[index].at[pl.ds(first, half), :], buffers[2].at[rows, lanes[index]])
                for index in range(3)
            ]
        )
    loads, count = [], 0
    for part in into:
        loads.append([])
        for source, buffer in part:
            loads[-1].append(pltpu.make_async_copy(source, buffer, in_sems.at[count]))
            count += 1
    stores = [
        pltpu.make_async_copy(buffer, target, out_sems.at[index])
        for index, (target, buffer) in enumerate(parts)
    ]
    for part in loads:
        for load in part:
            load.start()
    for part, store in zip(loads, stores):
        for load in part:
            load.wait()
        store.start()
    for store in stores:
        store.wait()


SCALAR = pl.BlockSpec(memory_space=pltpu.SMEM)
WHOLE = pl.BlockSpec(memory_space=pltpu.VMEM)


def tile_stats(ctx_index, query_blocks, key_blocks):
    tile = jax.ShapeDtypeStruct((TILE, 2 * WIDTH), jnp.bfloat16)
    return pl.pallas_call(
        stats_kernel,
        out_shape=[tile, tile, jax.ShapeDtypeStruct((8 * 24, WIDTH), jnp.float32)],
        in_specs=[SCALAR] + [WHOLE] * 16,
        out_specs=[WHOLE] * 3,
        compiler_params=pltpu.CompilerParams(vmem_limit_bytes=32 * 2**20),
        cost_estimate=pl.CostEstimate(
            flops=4 * 10 * QUARTER * QUARTER * WIDTH,
            bytes_accessed=4 * TILE * 4 * WIDTH,
            transcendentals=10 * QUARTER * QUARTER,
        ),
        name="tile_stats",
    )(ctx_index, *query_blocks, *key_blocks)


def tile_grads(ctx_index, queries, keys, stats):
    own = jax.ShapeDtypeStruct((4 * ROWS, 2 * WIDTH), jnp.float32)
    other = jax.ShapeDtypeStruct((4 * ROWS, 2 * WIDTH), jnp.bfloat16)
    pair = jax.ShapeDtypeStruct((QUARTER, WIDTH), jnp.bfloat16)
    first = jax.ShapeDtypeStruct((QUARTER, WIDTH), jnp.float32)
    outs = pl.pallas_call(
        grads_kernel,
        out_shape=[first] + [pair] * 3 + [own, other],
        in_specs=[SCALAR] + [WHOLE] * 3,
        out_specs=[WHOLE] * 6,
        scratch_shapes=[
            pltpu.VMEM((TILE, WIDTH), jnp.float32),
            pltpu.VMEM((TILE, 2 * WIDTH), jnp.float32),
            pltpu.VMEM((WIDTH, TILE), jnp.float32),
        ],
        compiler_params=pltpu.CompilerParams(vmem_limit_bytes=32 * 2**20),
        cost_estimate=pl.CostEstimate(
            flops=10 * 10 * QUARTER * QUARTER * WIDTH,
            bytes_accessed=4 * TILE * 4 * WIDTH,
            transcendentals=10 * QUARTER * QUARTER,
        ),
        name="tile_grads",
    )(ctx_index, queries, keys, stats)
    return outs[:4], outs[4], outs[5]


def pack(core, weights, blocks):
    rows = weights[0].shape[0] // 2
    shapes = [(ROWS, 2 * WIDTH), (ROWS, 2 * WIDTH), (rows, 3 * WIDTH)]
    anywhere = pl.BlockSpec(memory_space=pl.ANY)
    return pl.pallas_call(
        pack_kernel,
        out_shape=[jax.ShapeDtypeStruct(shape, jnp.bfloat16) for shape in shapes],
        in_specs=[SCALAR] + [anywhere] * 7,
        out_specs=[anywhere] * 3,
        scratch_shapes=[pltpu.VMEM(shape, jnp.bfloat16) for shape in shapes]
        + [pltpu.SemaphoreType.DMA((16,)), pltpu.SemaphoreType.DMA((6,))],
        compiler_params=pltpu.CompilerParams(vmem_limit_bytes=56 * 2**20),
        cost_estimate=pl.CostEstimate(
            flops=0, bytes_accessed=12 * rows * WIDTH, transcendentals=0
        ),
        name="pack",
    )(core, *weights, *blocks)


def rope_tables(first_row, length, head_width):
    halfway = head_width // 2
    indices = jnp.arange(halfway).astype(jnp.float32)
    frequency = jnp.exp(indices * (-2.0 * math.log(10000.0) / head_width))
    positions = (first_row + jnp.arange(length, dtype=jnp.int32)).astype(jnp.float32)
    angles = positions[:, None] * frequency[None, :]
    cosine = jnp.cos(angles)
    sine_part = jnp.sin(angles)
    return (
        jnp.concatenate([cosine, cosine], axis=1),
        jnp.concatenate([sine_part, sine_part], axis=1),
    )


def rope_back(gradient, cosine, sine_part):
    halfway = gradient.shape[1] // 2
    turned = gradient * sine_part
    return gradient * cosine + jnp.concatenate([turned[:, halfway:], -turned[:, :halfway]], axis=1)


def to_head(value, step):
    count = lax.axis_size("head")
    return lax.ppermute(value, "head", [(h, (h + step) % count) for h in range(count)])


def shards(queries, key_rows, value_rows, out_grads, query_proj, key_proj, value_proj):
    ctx_index = lax.axis_index("ctx")
    head = lax.axis_index("head")
    scalar = ctx_index.astype(jnp.int32).reshape(1)
    core = ctx_index % 2
    query_pair, key_pair, packed = pack(
        core.astype(jnp.int32).reshape(1),
        (query_proj, key_proj, value_proj),
        (queries, out_grads, key_rows, value_rows),
    )
    own_half = lax.all_to_all(packed, "head", 0, 0, tiled=True)
    query_near = to_neighbour(query_pair)
    near = {0: key_pair} | {st: to_key_member(key_pair, st) for st in STEPS}
    query_blocks = {(0, 0): query_pair, (0, 1): query_near}
    for se in range(2):
        for sx in STEPS:
            query_blocks[sx, se] = to_query_member(query_blocks[0, se], sx, 0)
    query_blocks = [query_blocks[shift] for shift in QUERY_SHIFTS]
    near = [near[st] for st in (0, 2, 1, 3)]
    key_blocks = near + [to_other_core(block) for block in near]

    query_blocks, own_half = lax.optimization_barrier((query_blocks, own_half))
    tile_queries, tile_keys, stats = tile_stats(scalar, query_blocks, key_blocks)

    stats, own_half = lax.optimization_barrier((stats, own_half))
    other_half = to_other_core(own_half)
    all_stats = exchange(stats, QUERY_GROUPS)
    all_stats, other_half = lax.optimization_barrier((all_stats, other_half))
    d_query_parts, own_part, other_part = tile_grads(scalar, tile_queries, tile_keys, all_stats)

    sums = own_part + to_other_core(other_part).astype(jnp.float32)
    d_pair = sums[:ROWS]
    for st in STEPS:
        sent = sums[st * ROWS : (st + 1) * ROWS].astype(jnp.bfloat16)
        d_pair = d_pair + to_key_member(sent, st).astype(jnp.float32)
    d_query_both = d_query_parts[0]
    for sx in STEPS:
        d_query_both = d_query_both + to_query_member(d_query_parts[sx], sx, 0).astype(jnp.float32)
    d_query = d_query_both[:ROWS] + to_neighbour(
        d_query_both[ROWS:].astype(jnp.bfloat16)
    ).astype(jnp.float32)
    cosine, sine_part = rope_tables(ctx_index * ROWS, ROWS, WIDTH)
    query_in = rope_back(d_query, cosine, sine_part).astype(jnp.bfloat16)
    key_in = rope_back(d_pair[:, :WIDTH], cosine, sine_part).astype(jnp.bfloat16)
    value_in = d_pair[:, WIDTH:].astype(jnp.bfloat16)
    grads = jnp.concatenate([query_in, key_in, value_in], axis=1)
    half_columns = own_half.shape[0] // 4
    totals = None
    for step in range(4):
        part = grads if step == 0 else to_head(grads, step)
        first = ((head + 4 - step) % 4) * half_columns
        terms = [
            lax.dot_general(
                part,
                lax.dynamic_slice_in_dim(half, first, half_columns, 0),
                CONTRACT_LAST,
                preferred_element_type=jnp.float32,
            )
            for half in (own_half, other_half)
        ]
        totals = terms if step == 0 else [total + term for total, term in zip(totals, terms)]
    own_out, other_out = [total.astype(jnp.bfloat16) for total in totals]
    return jnp.where(
        core == 0,
        jnp.concatenate([own_out, other_out], axis=1),
        jnp.concatenate([other_out, own_out], axis=1),
    )


def solution(mesh):
    in_specs = (P("ctx", "head"),) * 4 + (P(None, "head"),) * 3
    return jax.shard_map(
        shards, mesh=mesh, in_specs=in_specs, out_specs=P("ctx", "head"), check_vma=False
    )
```

profile of v0, /device:TPU:1, one launch (start us, length us, event | category | flops | bytes accessed | tf_op | source)
XLA Modules:
  0.0 85.5 jit_solution(1605957355523537410)
XLA Ops:
  0.0 2.6 %pack.1 = (bf16[192,256]{1,0:T(8,128)(2,1)}, bf16[192,256]{1,0:T(8,128)(2,1)}, bf16[2560,384]{1,0:T(8,128)(2,1)}) custom-call(s32[1]{0:T(128)} %bitcast.1.core_ref, bf16[5120,128]{1,0:T(8,128)(2,1)} %refs_0_.1, bf16[5120,128]{1,0:T(8,128)(2,1)} %refs_1_.1, bf16[5120,128]{1,0:T(8,128)(2,1)} %refs_2_.1, bf16[192,128]{1,0:T(8,128)(2,1)} %refs_3_.1, ...), custom_call_target="tpu_custom_call" | custom-call | bytes 3932160 | tf_op jit(solution)/shard_map/pack/pallas_call | solution.py:283
  2.7 5.2 %all-to-all-start = ((bf16[4,640,384]{2,1,0:T(8,128)(2,1)}), bf16[4,640,384]{2,1,0:T(8,128)(2,1)S(1)}, u32[]{:S(2)}, u32[]{:S(2)}) async-start(bf16[4,640,384]{2,1,0:T(8,128)(2,1)} %bitcast.19), calls=%async_computation | async-start | bytes 3932160 | tf_op jit(solution)/shard_map/all_to_all | solution.py:333
  7.8 1.6 %collective-permute-start = (bf16[192,256]{1,0:T(8,128)(2,1)S(1)}, bf16[192,256]{1,0:T(8,128)(2,1)S(1)}, u32[]{:S(2)}, u32[]{:S(2)}) collective-permute-start(bf16[192,256]{1,0:T(8,128)(2,1)S(1)} %copy-done), channel_id=1, source_target_pairs={{0,8},{4,12},{8,0},{12,4},{16,24},{20,28},{24,16},{28,20},{32,40},... | collective-permute-start | bytes 294920 | tf_op jit(solution)/shard_map/ppermute | solution.py:43
  9.5 1.2 %collective-permute-start.1 = (bf16[192,256]{1,0:T(8,128)(2,1)S(1)}, bf16[192,256]{1,0:T(8,128)(2,1)S(1)}, u32[]{:S(2)}, u32[]{:S(2)}) collective-permute-start(bf16[192,256]{1,0:T(8,128)(2,1)S(1)} %copy-done), channel_id=1, source_target_pairs={{0,64},{4,68},{8,72},{12,76},{16,80},{20,84},{24,88},{28,92},{32,9... | collective-permute-start | bytes 294920 | tf_op jit(solution)/shard_map/ppermute | solution.py:43
  10.7 2.5 %collective-permute-start.3 = (bf16[192,256]{1,0:T(8,128)(2,1)S(1)}, bf16[192,256]{1,0:T(8,128)(2,1)S(1)}, u32[]{:S(2)}, u32[]{:S(2)}) collective-permute-start(bf16[192,256]{1,0:T(8,128)(2,1)S(1)} %copy-done), channel_id=1, source_target_pairs={{0,128},{4,132},{8,136},{12,140},{16,144},{20,148},{24,152},{28,15... | collective-permute-start | bytes 294920 | tf_op jit(solution)/shard_map/ppermute | solution.py:43
  13.3 7.3 %collective-permute-start.7 = (bf16[192,256]{1,0:T(8,128)(2,1)S(1)}, bf16[192,256]{1,0:T(8,128)(2,1)S(1)}, u32[]{:S(2)}, u32[]{:S(2)}) collective-permute-start(bf16[192,256]{1,0:T(8,128)(2,1)S(1)} %copy-done.1), channel_id=1, source_target_pairs={{0,160},{4,164},{8,168},{12,172},{16,176},{20,180},{24,184},{28,18... | collective-permute-start | bytes 294920 | tf_op jit(solution)/shard_map/ppermute | solution.py:47
  20.6 2.4 %collective-permute-start.8 = (bf16[192,256]{1,0:T(8,128)(2,1)S(1)}, bf16[192,256]{1,0:T(8,128)(2,1)S(1)}, u32[]{:S(2)}, u32[]{:S(2)}) collective-permute-start(bf16[192,256]{1,0:T(8,128)(2,1)S(1)} %copy-done.1), channel_id=1, source_target_pairs={{0,80},{4,84},{8,88},{12,92},{16,192},{20,196},{24,200},{28,204},{... | collective-permute-start | bytes 294920 | tf_op jit(solution)/shard_map/ppermute | solution.py:47
  23.2 2.3 %collective-permute-start.4 = (bf16[192,256]{1,0:T(8,128)(2,1)S(1)}, bf16[192,256]{1,0:T(8,128)(2,1)S(1)}, u32[]{:S(2)}, u32[]{:S(2)}) collective-permute-start(bf16[192,256]{1,0:T(8,128)(2,1)S(1)} %collective-permute-done.refs_1_), channel_id=1, source_target_pairs={{0,128},{4,132},{8,136},{12,140},{16,144},{20,148},{24,152},{28,15... | collective-permute-start | bytes 294920 | tf_op jit(solution)/shard_map/ppermute | solution.py:43
  25.5 1.5 %collective-permute-start.6 = (bf16[192,256]{1,0:T(8,128)(2,1)S(1)}, bf16[192,256]{1,0:T(8,128)(2,1)S(1)}, u32[]{:S(2)}, u32[]{:S(2)}) collective-permute-start(bf16[192,256]{1,0:T(8,128)(2,1)S(1)} %collective-permute-done.refs_1_), channel_id=1, source_target_pairs={{0,192},{4,196},{8,200},{12,204},{16,208},{20,212},{24,216},{28,22... | collective-permute-start | bytes 294920 | tf_op jit(solution)/shard_map/ppermute | solution.py:43
  27.0 4.9 %collective-permute-done.8.refs_10_ = bf16[192,256]{1,0:T(8,128)(2,1)S(1)} collective-permute-done((bf16[192,256]{1,0:T(8,128)(2,1)S(1)}, bf16[192,256]{1,0:T(8,128)(2,1)S(1)}, u32[]{:S(2)}, u32[]{:S(2)}) %collective-permute-start.8) | collective-permute-done | bytes 98336 | tf_op jit(solution)/shard_map/ppermute | solution.py:47
  32.4 2.4 %collective-permute-start.11 = (bf16[192,256]{1,0:T(8,128)(2,1)S(1)}, bf16[192,256]{1,0:T(8,128)(2,1)S(1)}, u32[]{:S(2)}, u32[]{:S(2)}) collective-permute-start(bf16[192,256]{1,0:T(8,128)(2,1)S(1)} %collective-permute-done.7.refs_9_), channel_id=1, source_target_pairs={{0,4},{4,0},{8,12},{12,8},{16,20},{20,16},{24,28},{28,24},{32,36},... | collective-permute-start | bytes 294920 | tf_op jit(solution)/shard_map/ppermute | solution.py:51
  36.3 2.3 %tile_stats.1 = (bf16[1536,256]{1,0:T(8,128)(2,1)S(1)}, bf16[1536,256]{1,0:T(8,128)(2,1)S(1)}, f32[192,128]{1,0:T(8,128)S(1)}) custom-call(s32[1]{0:T(128)} %bitcast.ctx_ref, bf16[192,256]{1,0:T(8,128)(2,1)S(1)} %copy-done, bf16[192,256]{1,0:T(8,128)(2,1)S(1)} %collective-permute-done.refs_1_, bf16[192,256]{1,0:T(8,128)(2,1)S(1)} %collective-permute-done.1.refs_2_, ...), custom_call_target="tpu_custom_call" | custom-call | flops 754974720 | bytes 3145728 | tf_op jit(solution)/shard_map/tile_stats/pallas_call | solution.py:238
  39.0 8.2 %all_to_all.24 = f32[8,24,128]{2,1,0:T(8,128)S(1)} all-to-all(f32[8,24,128]{2,1,0:T(8,128)S(1)} %bitcast.12), channel_id=1, replica_groups={{0,8,64,72,128,136,192,200},{4,12,68,76,132,140,196,204},{16,24,80,88,1..., dimensions={0} | all-to-all | bytes 196608 | tf_op jit(solution)/shard_map/all_to_all | solution.py:60
  47.2 4.2 %tile_grads.1 = (f32[384,128]{1,0:T(8,128)S(1)}, bf16[384,128]{1,0:T(8,128)(2,1)S(1)}, bf16[384,128]{1,0:T(8,128)(2,1)S(1)}, bf16[384,128]{1,0:T(8,128)(2,1)S(1)...) custom-call(s32[1]{0:T(128)} %bitcast.ctx_ref, bf16[1536,256]{1,0:T(8,128)(2,1)S(1)} %get-tuple-element.41.query_ref, ...), custom_call_target="tpu_custom_call" | custom-call | flops 1887436800 | bytes 3145728 | tf_op jit(solution)/shard_map/tile_grads/pallas_call | solution.py:258
  51.4 1.5 %collective-permute-start.19 = (bf16[768,256]{1,0:T(8,128)(2,1)S(1)}, bf16[768,256]{1,0:T(8,128)(2,1)S(1)}, u32[]{:S(2)}, u32[]{:S(2)}) collective-permute-start(bf16[768,256]{1,0:T(8,128)(2,1)S(1)} %get-tuple-element.53), channel_id=1, source_target_pairs={{0,4},{4,0},{8,12},{12,8},{16,20},{20,16},{24,28},{28,24},{32,36},... | collective-permute-start | bytes 1179656 | tf_op jit(solution)/shard_map/ppermute | solution.py:51
  54.9 1.9 %collective-permute-start.17 = (bf16[384,128]{1,0:T(8,128)(2,1)S(1)}, bf16[384,128]{1,0:T(8,128)(2,1)S(1)}, u32[]{:S(2)}, u32[]{:S(2)}) collective-permute-start(bf16[384,128]{1,0:T(8,128)(2,1)S(1)} %get-tuple-element.51), channel_id=1, source_target_pairs={{0,192},{4,196},{8,200},{12,204},{16,208},{20,212},{24,216},{28,22... | collective-permute-start | bytes 294920 | tf_op jit(solution)/shard_map/ppermute | solution.py:43
  56.9 6.3 %collective-permute-start.20 = (bf16[192,256]{1,0:T(8,128)(2,1)S(1)}, bf16[192,256]{1,0:T(8,128)(2,1)S(1)}, u32[]{:S(2)}, u32[]{:S(2)}) collective-permute-start(bf16[192,256]{1,0:T(8,128)(2,1)S(1)} %get-tuple-element.57), channel_id=1, source_target_pairs={{0,160},{4,164},{8,168},{12,172},{16,176},{20,180},{24,184},{28,18... | collective-permute-start | bytes 294920 | tf_op jit(solution)/shard_map/ppermute | solution.py:47
  63.2 1.3 %collective-permute-start.21 = (bf16[192,256]{1,0:T(8,128)(2,1)S(1)}, bf16[192,256]{1,0:T(8,128)(2,1)S(1)}, u32[]{:S(2)}, u32[]{:S(2)}) collective-permute-start(bf16[192,256]{1,0:T(8,128)(2,1)S(1)} %get-tuple-element.59), channel_id=1, source_target_pairs={{0,80},{4,84},{8,88},{12,92},{16,192},{20,196},{24,200},{28,204},{... | collective-permute-start | bytes 294920 | tf_op jit(solution)/shard_map/ppermute | solution.py:47
  65.6 1.2 %collective-permute-done.20 = bf16[192,256]{1,0:T(8,128)(2,1)S(1)} collective-permute-done((bf16[192,256]{1,0:T(8,128)(2,1)S(1)}, bf16[192,256]{1,0:T(8,128)(2,1)S(1)}, u32[]{:S(2)}, u32[]{:S(2)}) %collective-permute-start.20) | collective-permute-done | bytes 98336 | tf_op jit(solution)/shard_map/ppermute | solution.py:47
  66.8 6.5 %collective-permute-done.21 = bf16[192,256]{1,0:T(8,128)(2,1)S(1)} collective-permute-done((bf16[192,256]{1,0:T(8,128)(2,1)S(1)}, bf16[192,256]{1,0:T(8,128)(2,1)S(1)}, u32[]{:S(2)}, u32[]{:S(2)}) %collective-permute-start.21) | collective-permute-done | bytes 98336 | tf_op jit(solution)/shard_map/ppermute | solution.py:47
  75.3 1.8 %collective-permute-start.25 = (bf16[192,384]{1,0:T(8,128)(2,1)S(1)}, bf16[192,384]{1,0:T(8,128)(2,1)S(1)}, u32[]{:S(2)}, u32[]{:S(2)}) collective-permute-start(bf16[192,384]{1,0:T(8,128)(2,1)S(1)} %pad_maximum_fusion), channel_id=1, source_target_pairs={{0,3},{1,0},{2,1},{3,2},{4,7},{5,4},{6,5},{7,6},{8,11},{9,8},{10,9... | collective-permute-start | bytes 442376 | tf_op jit(solution)/shard_map/ppermute | solution.py:320
  77.1 1.1 %collective-permute-start.24 = (bf16[192,384]{1,0:T(8,128)(2,1)S(1)}, bf16[192,384]{1,0:T(8,128)(2,1)S(1)}, u32[]{:S(2)}, u32[]{:S(2)}) collective-permute-start(bf16[192,384]{1,0:T(8,128)(2,1)S(1)} %pad_maximum_fusion), channel_id=1, source_target_pairs={{0,2},{1,3},{2,0},{3,1},{4,6},{5,7},{6,4},{7,5},{8,10},{9,11},{10,... | collective-permute-start | bytes 442376 | tf_op jit(solution)/shard_map/ppermute | solution.py:320
  78.6 1.1 %collective-permute-done.23 = bf16[192,384]{1,0:T(8,128)(2,1)S(1)} collective-permute-done((bf16[192,384]{1,0:T(8,128)(2,1)S(1)}, bf16[192,384]{1,0:T(8,128)(2,1)S(1)}, u32[]{:S(2)}, u32[]{:S(2)}) %collective-permute-start.23) | collective-permute-done | bytes 147488 | tf_op jit(solution)/shard_map/ppermute | solution.py:320
  81.6 2.2 %collective-permute-done.24 = bf16[192,384]{1,0:T(8,128)(2,1)S(1)} collective-permute-done((bf16[192,384]{1,0:T(8,128)(2,1)S(1)}, bf16[192,384]{1,0:T(8,128)(2,1)S(1)}, u32[]{:S(2)}, u32[]{:S(2)}) %collective-permute-start.24) | collective-permute-done | bytes 147488 | tf_op jit(solution)/shard_map/ppermute | solution.py:320
  (68 shorter events, 11.7 us)
Async XLA Ops:
  2.7 32.6 %all-to-all-start = ((bf16[4,640,384]{2,1,0:T(8,128)(2,1)}), bf16[4,640,384]{2,1,0:T(8,128)(2,1)S(1)}, u32[]{:S(2)}, u32[]{:S(2)}) async-start(bf16[4,640,384]{2,1,0:T(8,128)(2,1)} %bitcast.19), calls=%async_computation | async-start | bytes 3932160 | tf_op jit(solution)/shard_map/all_to_all | solution.py:333
  7.8 12.8 %collective-permute-start = (bf16[192,256]{1,0:T(8,128)(2,1)S(1)}, bf16[192,256]{1,0:T(8,128)(2,1)S(1)}, u32[]{:S(2)}, u32[]{:S(2)}) collective-permute-start(bf16[192,256]{1,0:T(8,128)(2,1)S(1)} %copy-done), channel_id=1, source_target_pairs={{0,8},{4,12},{8,0},{12,4},{16,24},{20,28},{24,16},{28,20},{32,40},... | collective-permute-start | bytes 294920 | tf_op jit(solution)/shard_map/ppermute | solution.py:43
  9.5 13.6 %collective-permute-start.1 = (bf16[192,256]{1,0:T(8,128)(2,1)S(1)}, bf16[192,256]{1,0:T(8,128)(2,1)S(1)}, u32[]{:S(2)}, u32[]{:S(2)}) collective-permute-start(bf16[192,256]{1,0:T(8,128)(2,1)S(1)} %copy-done), channel_id=1, source_target_pairs={{0,64},{4,68},{8,72},{12,76},{16,80},{20,84},{24,88},{28,92},{32,9... | collective-permute-start | bytes 294920 | tf_op jit(solution)/shard_map/ppermute | solution.py:43
  10.7 12.4 %collective-permute-start.3 = (bf16[192,256]{1,0:T(8,128)(2,1)S(1)}, bf16[192,256]{1,0:T(8,128)(2,1)S(1)}, u32[]{:S(2)}, u32[]{:S(2)}) collective-permute-start(bf16[192,256]{1,0:T(8,128)(2,1)S(1)} %copy-done), channel_id=1, source_target_pairs={{0,128},{4,132},{8,136},{12,140},{16,144},{20,148},{24,152},{28,15... | collective-permute-start | bytes 294920 | tf_op jit(solution)/shard_map/ppermute | solution.py:43
  13.1 10.0 %collective-permute-start.5 = (bf16[192,256]{1,0:T(8,128)(2,1)S(1)}, bf16[192,256]{1,0:T(8,128)(2,1)S(1)}, u32[]{:S(2)}, u32[]{:S(2)}) collective-permute-start(bf16[192,256]{1,0:T(8,128)(2,1)S(1)} %copy-done), channel_id=1, source_target_pairs={{0,192},{4,196},{8,200},{12,204},{16,208},{20,212},{24,216},{28,22... | collective-permute-start | bytes 294920 | tf_op jit(solution)/shard_map/ppermute | solution.py:43
  13.3 12.1 %collective-permute-start.7 = (bf16[192,256]{1,0:T(8,128)(2,1)S(1)}, bf16[192,256]{1,0:T(8,128)(2,1)S(1)}, u32[]{:S(2)}, u32[]{:S(2)}) collective-permute-start(bf16[192,256]{1,0:T(8,128)(2,1)S(1)} %copy-done.1), channel_id=1, source_target_pairs={{0,160},{4,164},{8,168},{12,172},{16,176},{20,180},{24,184},{28,18... | collective-permute-start | bytes 294920 | tf_op jit(solution)/shard_map/ppermute | solution.py:47
  20.6 11.3 %collective-permute-start.8 = (bf16[192,256]{1,0:T(8,128)(2,1)S(1)}, bf16[192,256]{1,0:T(8,128)(2,1)S(1)}, u32[]{:S(2)}, u32[]{:S(2)}) collective-permute-start(bf16[192,256]{1,0:T(8,128)(2,1)S(1)} %copy-done.1), channel_id=1, source_target_pairs={{0,80},{4,84},{8,88},{12,92},{16,192},{20,196},{24,200},{28,204},{... | collective-permute-start | bytes 294920 | tf_op jit(solution)/shard_map/ppermute | solution.py:47
  23.0 9.4 %collective-permute-start.9 = (bf16[192,256]{1,0:T(8,128)(2,1)S(1)}, bf16[192,256]{1,0:T(8,128)(2,1)S(1)}, u32[]{:S(2)}, u32[]{:S(2)}) collective-permute-start(bf16[192,256]{1,0:T(8,128)(2,1)S(1)} %copy-done.1), channel_id=1, source_target_pairs={{0,240},{4,244},{8,248},{12,252},{16,96},{20,100},{24,104},{28,108... | collective-permute-start | bytes 294920 | tf_op jit(solution)/shard_map/ppermute | solution.py:47
  23.0 11.8 %collective-permute-start.2 = (bf16[192,256]{1,0:T(8,128)(2,1)S(1)}, bf16[192,256]{1,0:T(8,128)(2,1)S(1)}, u32[]{:S(2)}, u32[]{:S(2)}) collective-permute-start(bf16[192,256]{1,0:T(8,128)(2,1)S(1)} %collective-permute-done.refs_1_), channel_id=1, source_target_pairs={{0,64},{4,68},{8,72},{12,76},{16,80},{20,84},{24,88},{28,92},{32,9... | collective-permute-start | bytes 294920 | tf_op jit(solution)/shard_map/ppermute | solution.py:43
  23.2 11.7 %collective-permute-start.4 = (bf16[192,256]{1,0:T(8,128)(2,1)S(1)}, bf16[192,256]{1,0:T(8,128)(2,1)S(1)}, u32[]{:S(2)}, u32[]{:S(2)}) collective-permute-start(bf16[192,256]{1,0:T(8,128)(2,1)S(1)} %collective-permute-done.refs_1_), channel_id=1, source_target_pairs={{0,128},{4,132},{8,136},{12,140},{16,144},{20,148},{24,152},{28,15... | collective-permute-start | bytes 294920 | tf_op jit(solution)/shard_map/ppermute | solution.py:43
  25.5 9.8 %collective-permute-start.6 = (bf16[192,256]{1,0:T(8,128)(2,1)S(1)}, bf16[192,256]{1,0:T(8,128)(2,1)S(1)}, u32[]{:S(2)}, u32[]{:S(2)}) collective-permute-start(bf16[192,256]{1,0:T(8,128)(2,1)S(1)} %collective-permute-done.refs_1_), channel_id=1, source_target_pairs={{0,192},{4,196},{8,200},{12,204},{16,208},{20,212},{24,216},{28,22... | collective-permute-start | bytes 294920 | tf_op jit(solution)/shard_map/ppermute | solution.py:43
  31.9 3.4 %collective-permute-start.10 = (bf16[192,256]{1,0:T(8,128)(2,1)S(1)}, bf16[192,256]{1,0:T(8,128)(2,1)S(1)}, u32[]{:S(2)}, u32[]{:S(2)}) collective-permute-start(bf16[192,256]{1,0:T(8,128)(2,1)S(1)} %copy-done.1), channel_id=1, source_target_pairs={{0,4},{4,0},{8,12},{12,8},{16,20},{20,16},{24,28},{28,24},{32,36},... | collective-permute-start | bytes 294920 | tf_op jit(solution)/shard_map/ppermute | solution.py:51
  38.6 8.6 %collective-permute-start.14 = (bf16[2560,384]{1,0:T(8,128)(2,1)S(1)}, bf16[2560,384]{1,0:T(8,128)(2,1)S(1)}, u32[]{:S(2)}, u32[]{:S(2)}) collective-permute-start(bf16[2560,384]{1,0:T(8,128)(2,1)S(1)} %bitcast.14), channel_id=1, source_target_pairs={{0,4},{4,0},{8,12},{12,8},{16,20},{20,16},{24,28},{28,24},{32,36},... | collective-permute-start | bytes 5898248 | tf_op jit(solution)/shard_map/ppermute | solution.py:51
  51.4 5.3 %collective-permute-start.19 = (bf16[768,256]{1,0:T(8,128)(2,1)S(1)}, bf16[768,256]{1,0:T(8,128)(2,1)S(1)}, u32[]{:S(2)}, u32[]{:S(2)}) collective-permute-start(bf16[768,256]{1,0:T(8,128)(2,1)S(1)} %get-tuple-element.53), channel_id=1, source_target_pairs={{0,4},{4,0},{8,12},{12,8},{16,20},{20,16},{24,28},{28,24},{32,36},... | collective-permute-start | bytes 1179656 | tf_op jit(solution)/shard_map/ppermute | solution.py:51
  53.4 11.1 %collective-permute-start.15 = (bf16[384,128]{1,0:T(8,128)(2,1)S(1)}, bf16[384,128]{1,0:T(8,128)(2,1)S(1)}, u32[]{:S(2)}, u32[]{:S(2)}) collective-permute-start(bf16[384,128]{1,0:T(8,128)(2,1)S(1)} %get-tuple-element.49), channel_id=1, source_target_pairs={{0,128},{4,132},{8,136},{12,140},{16,144},{20,148},{24,152},{28,15... | collective-permute-start | bytes 294920 | tf_op jit(solution)/shard_map/ppermute | solution.py:43
  54.4 10.6 %collective-permute-start.16 = (bf16[384,128]{1,0:T(8,128)(2,1)S(1)}, bf16[384,128]{1,0:T(8,128)(2,1)S(1)}, u32[]{:S(2)}, u32[]{:S(2)}) collective-permute-start(bf16[384,128]{1,0:T(8,128)(2,1)S(1)} %get-tuple-element.50), channel_id=1, source_target_pairs={{0,64},{4,68},{8,72},{12,76},{16,80},{20,84},{24,88},{28,92},{32,9... | collective-permute-start | bytes 294920 | tf_op jit(solution)/shard_map/ppermute | solution.py:43
  54.9 10.2 %collective-permute-start.17 = (bf16[384,128]{1,0:T(8,128)(2,1)S(1)}, bf16[384,128]{1,0:T(8,128)(2,1)S(1)}, u32[]{:S(2)}, u32[]{:S(2)}) collective-permute-start(bf16[384,128]{1,0:T(8,128)(2,1)S(1)} %get-tuple-element.51), channel_id=1, source_target_pairs={{0,192},{4,196},{8,200},{12,204},{16,208},{20,212},{24,216},{28,22... | collective-permute-start | bytes 294920 | tf_op jit(solution)/shard_map/ppermute | solution.py:43
  56.9 9.9 %collective-permute-start.20 = (bf16[192,256]{1,0:T(8,128)(2,1)S(1)}, bf16[192,256]{1,0:T(8,128)(2,1)S(1)}, u32[]{:S(2)}, u32[]{:S(2)}) collective-permute-start(bf16[192,256]{1,0:T(8,128)(2,1)S(1)} %get-tuple-element.57), channel_id=1, source_target_pairs={{0,160},{4,164},{8,168},{12,172},{16,176},{20,180},{24,184},{28,18... | collective-permute-start | bytes 294920 | tf_op jit(solution)/shard_map/ppermute | solution.py:47
  63.2 10.1 %collective-permute-start.21 = (bf16[192,256]{1,0:T(8,128)(2,1)S(1)}, bf16[192,256]{1,0:T(8,128)(2,1)S(1)}, u32[]{:S(2)}, u32[]{:S(2)}) collective-permute-start(bf16[192,256]{1,0:T(8,128)(2,1)S(1)} %get-tuple-element.59), channel_id=1, source_target_pairs={{0,80},{4,84},{8,88},{12,92},{16,192},{20,196},{24,200},{28,204},{... | collective-permute-start | bytes 294920 | tf_op jit(solution)/shard_map/ppermute | solution.py:47
  64.5 9.1 %collective-permute-start.22 = (bf16[192,256]{1,0:T(8,128)(2,1)S(1)}, bf16[192,256]{1,0:T(8,128)(2,1)S(1)}, u32[]{:S(2)}, u32[]{:S(2)}) collective-permute-start(bf16[192,256]{1,0:T(8,128)(2,1)S(1)} %get-tuple-element.58), channel_id=1, source_target_pairs={{0,240},{4,244},{8,248},{12,252},{16,96},{20,100},{24,104},{28,108... | collective-permute-start | bytes 294920 | tf_op jit(solution)/shard_map/ppermute | solution.py:47
  65.1 8.8 %collective-permute-start.18 = (bf16[192,128]{1,0:T(8,128)(2,1)S(1)}, bf16[192,128]{1,0:T(8,128)(2,1)S(1)}, u32[]{:S(2)}, u32[]{:S(2)}) collective-permute-start(bf16[192,128]{1,0:T(8,128)(2,1)S(1)} %slice.82), channel_id=1, source_target_pairs={{0,8},{4,12},{8,0},{12,4},{16,24},{20,28},{24,16},{28,20},{32,40},... | collective-permute-start | bytes 147464 | tf_op jit(solution)/shard_map/ppermute | solution.py:43
  74.3 5.3 %collective-permute-start.23 = (bf16[192,384]{1,0:T(8,128)(2,1)S(1)}, bf16[192,384]{1,0:T(8,128)(2,1)S(1)}, u32[]{:S(2)}, u32[]{:S(2)}) collective-permute-start(bf16[192,384]{1,0:T(8,128)(2,1)S(1)} %pad_maximum_fusion), channel_id=1, source_target_pairs={{0,1},{1,2},{2,3},{3,0},{4,5},{5,6},{6,7},{7,4},{8,9},{9,10},{10,1... | collective-permute-start | bytes 442376 | tf_op jit(solution)/shard_map/ppermute | solution.py:320
  75.3 5.6 %collective-permute-start.25 = (bf16[192,384]{1,0:T(8,128)(2,1)S(1)}, bf16[192,384]{1,0:T(8,128)(2,1)S(1)}, u32[]{:S(2)}, u32[]{:S(2)}) collective-permute-start(bf16[192,384]{1,0:T(8,128)(2,1)S(1)} %pad_maximum_fusion), channel_id=1, source_target_pairs={{0,3},{1,0},{2,1},{3,2},{4,7},{5,4},{6,5},{7,6},{8,11},{9,8},{10,9... | collective-permute-start | bytes 442376 | tf_op jit(solution)/shard_map/ppermute | solution.py:320
  77.1 6.7 %collective-permute-start.24 = (bf16[192,384]{1,0:T(8,128)(2,1)S(1)}, bf16[192,384]{1,0:T(8,128)(2,1)S(1)}, u32[]{:S(2)}, u32[]{:S(2)}) collective-permute-start(bf16[192,384]{1,0:T(8,128)(2,1)S(1)} %pad_maximum_fusion), channel_id=1, source_target_pairs={{0,2},{1,3},{2,0},{3,1},{4,6},{5,7},{6,4},{7,5},{8,10},{9,11},{10,... | collective-permute-start | bytes 442376 | tf_op jit(solution)/shard_map/ppermute | solution.py:320
  (9 other events, 55.9 us)
where the time goes:
time: 86.1 us; the launch traced here: 85.5 us
  starting transfers between devices  45.6 us (53%)
  waiting for transfers between devices  17.6 us (20%)
  Pallas kernels  9.18 us (11%)
  blocking collectives  8.16 us (9%)
  matrix products  2.79 us (3%)
  other arithmetic  1.9 us (2%)
    ppermute x6, starting transfers between devices, to_key_member(): lax.ppermute(value, 'ctx', pairs_of(lambda x, t, e, c: (x - t + (t ^ st),...  17.8 us
    ppermute x11, starting transfers between devices, to_query_member(): lax.ppermute(value, 'ctx', pairs_of(lambda x, t, e, c: (x ^ sx, t, e ^ se...  13.3 us
    ppermute x6, waiting for transfers between devices, to_key_member(): lax.ppermute(value, 'ctx', pairs_of(lambda x, t, e, c: (x - t + (t ^ st),...  12.9 us
    all_to_all x1, blocking collectives, exchange(): lax.all_to_all(value, 'ctx', 0, 0, axis_index_groups=groups, tiled=True)  8.16 us
    ppermute x6, starting transfers between devices, to_other_core(): lax.ppermute(value, 'ctx', pairs_of(lambda x, t, e, c: (x, t, e, 1 - c)))  5.39 us
    all_to_all x1, starting transfers between devices, shards(): own_half = lax.all_to_all(packed, 'head', 0, 0, tiled=True)  5.16 us
    pallas_call x1, Pallas kernels, tile_grads(): pl.pallas_call(grads_kernel, out_shape=[first] + [pair] * 3 + [own, other...  4.22 us
    ppermute x3, starting transfers between devices, to_head(): lax.ppermute(value, 'head', [(h, (h + step) % count) for h in range(count)])  3.87 us
  transfers between devices with their start and end apart: 27, of which 11 were waited for; matrix products, arithmetic and copies ran while one was open for 3% of the time, Pallas kernels for 0%

commit v1 on v0

--- a/solution.py
+++ b/solution.py
@@ -193,11 +193,7 @@
     buffers, (in_sems, out_sems) = refs[10:13], refs[13:]
     half = targets[2].shape[0] // 4
     lanes = [pl.ds(index * WIDTH, WIDTH) for index in range(3)]
-    parts = list(zip(targets, buffers))[:2]
-    into = [
-        [(sources[3 + 2 * pair + index], buffers[pair].at[:, lanes[index]]) for index in range(2)]
-        for pair in range(2)
-    ]
+    parts, into = [], []
     for owner in range(4):
         first = pl.multiple_of((2 * owner + core_ref[0]) * half, half)
         rows = pl.ds(owner * half, half)
@@ -208,6 +204,11 @@
                 for index in range(3)
             ]
         )
+    parts += list(zip(targets, buffers))[:2]
+    into += [
+        [(sources[3 + 2 * pair + index], buffers[pair].at[:, lanes[index]]) for index in range(2)]
+        for pair in range(2)
+    ]
     loads, count = [], 0
     for part in into:
         loads.append([])
@@ -350,11 +351,12 @@
     all_stats, other_half = lax.optimization_barrier((all_stats, other_half))
     d_query_parts, own_part, other_part = tile_grads(scalar, tile_queries, tile_keys, all_stats)
 
-    sums = own_part + to_other_core(other_part).astype(jnp.float32)
-    d_pair = sums[:ROWS]
+    from_core = to_other_core(other_part)
+    blocks = [slice(st * ROWS, (st + 1) * ROWS) for st in range(4)]
+    sums = [own_part[rows] + from_core[rows].astype(jnp.float32) for rows in blocks]
+    d_pair = sums[0]
     for st in STEPS:
-        sent = sums[st * ROWS : (st + 1) * ROWS].astype(jnp.bfloat16)
-        d_pair = d_pair + to_key_member(sent, st).astype(jnp.float32)
+        d_pair = d_pair + to_key_member(sums[st].astype(jnp.bfloat16), st).astype(jnp.float32)
     d_query_both = d_query_parts[0]
     for sx in STEPS:
         d_query_both = d_query_both + to_query_member(d_query_parts[sx], sx, 0).astype(jnp.float32)

time: 86.1 us -> 86 us (level)
  no operation moved by 1% of the time
where the time goes in v1:
time: 86 us; the launch traced here: 85.4 us
  starting transfers between devices  45.6 us (53%)
  waiting for transfers between devices  17.6 us (20%)
  Pallas kernels  9.18 us (11%)
  blocking collectives  8.16 us (9%)
  matrix products  2.79 us (3%)
  other arithmetic  1.88 us (2%)
    ppermute x6, starting transfers between devices, to_key_member(): lax.ppermute(value, 'ctx', pairs_of(lambda x, t, e, c: (x - t + (t ^ st),...  17.8 us
    ppermute x11, starting transfers between devices, to_query_member(): lax.ppermute(value, 'ctx', pairs_of(lambda x, t, e, c: (x ^ sx, t, e ^ se...  13.3 us
    ppermute x6, waiting for transfers between devices, to_key_member(): lax.ppermute(value, 'ctx', pairs_of(lambda x, t, e, c: (x - t + (t ^ st),...  12.9 us
    all_to_all x1, blocking collectives, exchange(): lax.all_to_all(value, 'ctx', 0, 0, axis_index_groups=groups, tiled=True)  8.16 us
    ppermute x6, starting transfers between devices, to_other_core(): lax.ppermute(value, 'ctx', pairs_of(lambda x, t, e, c: (x, t, e, 1 - c)))  5.38 us
    all_to_all x1, starting transfers between devices, shards(): own_half = lax.all_to_all(packed, 'head', 0, 0, tiled=True)  5.16 us
    pallas_call x1, Pallas kernels, tile_grads(): pl.pallas_call(grads_kernel, out_shape=[first] + [pair] * 3 + [own, other...  4.22 us
    ppermute x3, starting transfers between devices, to_head(): lax.ppermute(value, 'head', [(h, (h + step) % count) for h in range(count)])  3.88 us
  transfers between devices with their start and end apart: 27, of which 11 were waited for; matrix products, arithmetic and copies ran while one was open for 3% of the time, Pallas kernels for 0%

profile of v1, /device:TPU:1, one launch (start us, length us, event | category | flops | bytes accessed | tf_op | source)
XLA Modules:
  0.0 85.4 jit_solution(9971503778883489599)
XLA Ops:
  0.0 2.6 %pack.1 = (bf16[192,256]{1,0:T(8,128)(2,1)}, bf16[192,256]{1,0:T(8,128)(2,1)}, bf16[2560,384]{1,0:T(8,128)(2,1)}) custom-call(s32[1]{0:T(128)} %bitcast.1.core_ref, bf16[5120,128]{1,0:T(8,128)(2,1)} %refs_0_.1, bf16[5120,128]{1,0:T(8,128)(2,1)} %refs_1_.1, bf16[5120,128]{1,0:T(8,128)(2,1)} %refs_2_.1, bf16[192,128]{1,0:T(8,128)(2,1)} %refs_3_.1, ...), custom_call_target="tpu_custom_call" | custom-call | bytes 3932160 | tf_op jit(solution)/shard_map/pack/pallas_call | solution.py:284
  2.7 5.2 %all-to-all-start = ((bf16[4,640,384]{2,1,0:T(8,128)(2,1)}), bf16[4,640,384]{2,1,0:T(8,128)(2,1)S(1)}, u32[]{:S(2)}, u32[]{:S(2)}) async-start(bf16[4,640,384]{2,1,0:T(8,128)(2,1)} %bitcast.19), calls=%async_computation | async-start | bytes 3932160 | tf_op jit(solution)/shard_map/all_to_all | solution.py:334
  7.8 1.6 %collective-permute-start = (bf16[192,256]{1,0:T(8,128)(2,1)S(1)}, bf16[192,256]{1,0:T(8,128)(2,1)S(1)}, u32[]{:S(2)}, u32[]{:S(2)}) collective-permute-start(bf16[192,256]{1,0:T(8,128)(2,1)S(1)} %copy-done), channel_id=1, source_target_pairs={{0,8},{4,12},{8,0},{12,4},{16,24},{20,28},{24,16},{28,20},{32,40},... | collective-permute-start | bytes 294920 | tf_op jit(solution)/shard_map/ppermute | solution.py:43
  9.5 1.2 %collective-permute-start.1 = (bf16[192,256]{1,0:T(8,128)(2,1)S(1)}, bf16[192,256]{1,0:T(8,128)(2,1)S(1)}, u32[]{:S(2)}, u32[]{:S(2)}) collective-permute-start(bf16[192,256]{1,0:T(8,128)(2,1)S(1)} %copy-done), channel_id=1, source_target_pairs={{0,64},{4,68},{8,72},{12,76},{16,80},{20,84},{24,88},{28,92},{32,9... | collective-permute-start | bytes 294920 | tf_op jit(solution)/shard_map/ppermute | solution.py:43
  10.7 2.5 %collective-permute-start.3 = (bf16[192,256]{1,0:T(8,128)(2,1)S(1)}, bf16[192,256]{1,0:T(8,128)(2,1)S(1)}, u32[]{:S(2)}, u32[]{:S(2)}) collective-permute-start(bf16[192,256]{1,0:T(8,128)(2,1)S(1)} %copy-done), channel_id=1, source_target_pairs={{0,128},{4,132},{8,136},{12,140},{16,144},{20,148},{24,152},{28,15... | collective-permute-start | bytes 294920 | tf_op jit(solution)/shard_map/ppermute | solution.py:43
  13.3 7.3 %collective-permute-start.7 = (bf16[192,256]{1,0:T(8,128)(2,1)S(1)}, bf16[192,256]{1,0:T(8,128)(2,1)S(1)}, u32[]{:S(2)}, u32[]{:S(2)}) collective-permute-start(bf16[192,256]{1,0:T(8,128)(2,1)S(1)} %copy-done.1), channel_id=1, source_target_pairs={{0,160},{4,164},{8,168},{12,172},{16,176},{20,180},{24,184},{28,18... | collective-permute-start | bytes 294920 | tf_op jit(solution)/shard_map/ppermute | solution.py:47
  20.6 2.4 %collective-permute-start.8 = (bf16[192,256]{1,0:T(8,128)(2,1)S(1)}, bf16[192,256]{1,0:T(8,128)(2,1)S(1)}, u32[]{:S(2)}, u32[]{:S(2)}) collective-permute-start(bf16[192,256]{1,0:T(8,128)(2,1)S(1)} %copy-done.1), channel_id=1, source_target_pairs={{0,80},{4,84},{8,88},{12,92},{16,192},{20,196},{24,200},{28,204},{... | collective-permute-start | bytes 294920 | tf_op jit(solution)/shard_map/ppermute | solution.py:47
  23.1 2.3 %collective-permute-start.4 = (bf16[192,256]{1,0:T(8,128)(2,1)S(1)}, bf16[192,256]{1,0:T(8,128)(2,1)S(1)}, u32[]{:S(2)}, u32[]{:S(2)}) collective-permute-start(bf16[192,256]{1,0:T(8,128)(2,1)S(1)} %collective-permute-done.refs_1_), channel_id=1, source_target_pairs={{0,128},{4,132},{8,136},{12,140},{16,144},{20,148},{24,152},{28,15... | collective-permute-start | bytes 294920 | tf_op jit(solution)/shard_map/ppermute | solution.py:43
  25.5 1.5 %collective-permute-start.6 = (bf16[192,256]{1,0:T(8,128)(2,1)S(1)}, bf16[192,256]{1,0:T(8,128)(2,1)S(1)}, u32[]{:S(2)}, u32[]{:S(2)}) collective-permute-start(bf16[192,256]{1,0:T(8,128)(2,1)S(1)} %collective-permute-done.refs_1_), channel_id=1, source_target_pairs={{0,192},{4,196},{8,200},{12,204},{16,208},{20,212},{24,216},{28,22... | collective-permute-start | bytes 294920 | tf_op jit(solution)/shard_map/ppermute | solution.py:43
  27.0 4.9 %collective-permute-done.8.refs_10_ = bf16[192,256]{1,0:T(8,128)(2,1)S(1)} collective-permute-done((bf16[192,256]{1,0:T(8,128)(2,1)S(1)}, bf16[192,256]{1,0:T(8,128)(2,1)S(1)}, u32[]{:S(2)}, u32[]{:S(2)}) %collective-permute-start.8) | collective-permute-done | bytes 98336 | tf_op jit(solution)/shard_map/ppermute | solution.py:47
  32.4 2.4 %collective-permute-start.11 = (bf16[192,256]{1,0:T(8,128)(2,1)S(1)}, bf16[192,256]{1,0:T(8,128)(2,1)S(1)}, u32[]{:S(2)}, u32[]{:S(2)}) collective-permute-start(bf16[192,256]{1,0:T(8,128)(2,1)S(1)} %collective-permute-done.7.refs_9_), channel_id=1, source_target_pairs={{0,4},{4,0},{8,12},{12,8},{16,20},{20,16},{24,28},{28,24},{32,36},... | collective-permute-start | bytes 294920 | tf_op jit(solution)/shard_map/ppermute | solution.py:51
  36.3 2.3 %tile_stats.1 = (bf16[1536,256]{1,0:T(8,128)(2,1)S(1)}, bf16[1536,256]{1,0:T(8,128)(2,1)S(1)}, f32[192,128]{1,0:T(8,128)S(1)}) custom-call(s32[1]{0:T(128)} %bitcast.ctx_ref, bf16[192,256]{1,0:T(8,128)(2,1)S(1)} %copy-done, bf16[192,256]{1,0:T(8,128)(2,1)S(1)} %collective-permute-done.refs_1_, bf16[192,256]{1,0:T(8,128)(2,1)S(1)} %collective-permute-done.1.refs_2_, ...), custom_call_target="tpu_custom_call" | custom-call | flops 754974720 | bytes 3145728 | tf_op jit(solution)/shard_map/tile_stats/pallas_call | solution.py:239
  39.0 8.2 %all_to_all.24 = f32[8,24,128]{2,1,0:T(8,128)S(1)} all-to-all(f32[8,24,128]{2,1,0:T(8,128)S(1)} %bitcast.12), channel_id=1, replica_groups={{0,8,64,72,128,136,192,200},{4,12,68,76,132,140,196,204},{16,24,80,88,1..., dimensions={0} | all-to-all | bytes 196608 | tf_op jit(solution)/shard_map/all_to_all | solution.py:60
  47.2 4.2 %tile_grads.1 = (f32[384,128]{1,0:T(8,128)S(1)}, bf16[384,128]{1,0:T(8,128)(2,1)S(1)}, bf16[384,128]{1,0:T(8,128)(2,1)S(1)}, bf16[384,128]{1,0:T(8,128)(2,1)S(1)...) custom-call(s32[1]{0:T(128)} %bitcast.ctx_ref, bf16[1536,256]{1,0:T(8,128)(2,1)S(1)} %get-tuple-element.41.query_ref, ...), custom_call_target="tpu_custom_call" | custom-call | flops 1887436800 | bytes 3145728 | tf_op jit(solution)/shard_map/tile_grads/pallas_call | solution.py:259
  51.4 1.5 %collective-permute-start.19 = (bf16[768,256]{1,0:T(8,128)(2,1)S(1)}, bf16[768,256]{1,0:T(8,128)(2,1)S(1)}, u32[]{:S(2)}, u32[]{:S(2)}) collective-permute-start(bf16[768,256]{1,0:T(8,128)(2,1)S(1)} %get-tuple-element.53), channel_id=1, source_target_pairs={{0,4},{4,0},{8,12},{12,8},{16,20},{20,16},{24,28},{28,24},{32,36},... | collective-permute-start | bytes 1179656 | tf_op jit(solution)/shard_map/ppermute | solution.py:51
  54.8 1.9 %collective-permute-start.17 = (bf16[384,128]{1,0:T(8,128)(2,1)S(1)}, bf16[384,128]{1,0:T(8,128)(2,1)S(1)}, u32[]{:S(2)}, u32[]{:S(2)}) collective-permute-start(bf16[384,128]{1,0:T(8,128)(2,1)S(1)} %get-tuple-element.51), channel_id=1, source_target_pairs={{0,192},{4,196},{8,200},{12,204},{16,208},{20,212},{24,216},{28,22... | collective-permute-start | bytes 294920 | tf_op jit(solution)/shard_map/ppermute | solution.py:43
  56.8 6.3 %collective-permute-start.20 = (bf16[192,256]{1,0:T(8,128)(2,1)S(1)}, bf16[192,256]{1,0:T(8,128)(2,1)S(1)}, u32[]{:S(2)}, u32[]{:S(2)}) collective-permute-start(bf16[192,256]{1,0:T(8,128)(2,1)S(1)} %get-tuple-element.55), channel_id=1, source_target_pairs={{0,160},{4,164},{8,168},{12,172},{16,176},{20,180},{24,184},{28,18... | collective-permute-start | bytes 294920 | tf_op jit(solution)/shard_map/ppermute | solution.py:47
  63.1 1.4 %collective-permute-start.21 = (bf16[192,256]{1,0:T(8,128)(2,1)S(1)}, bf16[192,256]{1,0:T(8,128)(2,1)S(1)}, u32[]{:S(2)}, u32[]{:S(2)}) collective-permute-start(bf16[192,256]{1,0:T(8,128)(2,1)S(1)} %get-tuple-element.57), channel_id=1, source_target_pairs={{0,80},{4,84},{8,88},{12,92},{16,192},{20,196},{24,200},{28,204},{... | collective-permute-start | bytes 294920 | tf_op jit(solution)/shard_map/ppermute | solution.py:47
  65.6 1.2 %collective-permute-done.20 = bf16[192,256]{1,0:T(8,128)(2,1)S(1)} collective-permute-done((bf16[192,256]{1,0:T(8,128)(2,1)S(1)}, bf16[192,256]{1,0:T(8,128)(2,1)S(1)}, u32[]{:S(2)}, u32[]{:S(2)}) %collective-permute-start.20) | collective-permute-done | bytes 98336 | tf_op jit(solution)/shard_map/ppermute | solution.py:47
  66.7 6.5 %collective-permute-done.21 = bf16[192,256]{1,0:T(8,128)(2,1)S(1)} collective-permute-done((bf16[192,256]{1,0:T(8,128)(2,1)S(1)}, bf16[192,256]{1,0:T(8,128)(2,1)S(1)}, u32[]{:S(2)}, u32[]{:S(2)}) %collective-permute-start.21) | collective-permute-done | bytes 98336 | tf_op jit(solution)/shard_map/ppermute | solution.py:47
  75.2 1.8 %collective-permute-start.25 = (bf16[192,384]{1,0:T(8,128)(2,1)S(1)}, bf16[192,384]{1,0:T(8,128)(2,1)S(1)}, u32[]{:S(2)}, u32[]{:S(2)}) collective-permute-start(bf16[192,384]{1,0:T(8,128)(2,1)S(1)} %pad_maximum_fusion), channel_id=1, source_target_pairs={{0,3},{1,0},{2,1},{3,2},{4,7},{5,4},{6,5},{7,6},{8,11},{9,8},{10,9... | collective-permute-start | bytes 442376 | tf_op jit(solution)/shard_map/ppermute | solution.py:321
  77.0 1.1 %collective-permute-start.24 = (bf16[192,384]{1,0:T(8,128)(2,1)S(1)}, bf16[192,384]{1,0:T(8,128)(2,1)S(1)}, u32[]{:S(2)}, u32[]{:S(2)}) collective-permute-start(bf16[192,384]{1,0:T(8,128)(2,1)S(1)} %pad_maximum_fusion), channel_id=1, source_target_pairs={{0,2},{1,3},{2,0},{3,1},{4,6},{5,7},{6,4},{7,5},{8,10},{9,11},{10,... | collective-permute-start | bytes 442376 | tf_op jit(solution)/shard_map/ppermute | solution.py:321
  78.5 1.1 %collective-permute-done.23 = bf16[192,384]{1,0:T(8,128)(2,1)S(1)} collective-permute-done((bf16[192,384]{1,0:T(8,128)(2,1)S(1)}, bf16[192,384]{1,0:T(8,128)(2,1)S(1)}, u32[]{:S(2)}, u32[]{:S(2)}) %collective-permute-start.23) | collective-permute-done | bytes 147488 | tf_op jit(solution)/shard_map/ppermute | solution.py:321
  81.5 2.3 %collective-permute-done.24 = bf16[192,384]{1,0:T(8,128)(2,1)S(1)} collective-permute-done((bf16[192,384]{1,0:T(8,128)(2,1)S(1)}, bf16[192,384]{1,0:T(8,128)(2,1)S(1)}, u32[]{:S(2)}, u32[]{:S(2)}) %collective-permute-start.24) | collective-permute-done | bytes 147488 | tf_op jit(solution)/shard_map/ppermute | solution.py:321
  (67 shorter events, 11.6 us)
Async XLA Ops:
  2.7 32.6 %all-to-all-start = ((bf16[4,640,384]{2,1,0:T(8,128)(2,1)}), bf16[4,640,384]{2,1,0:T(8,128)(2,1)S(1)}, u32[]{:S(2)}, u32[]{:S(2)}) async-start(bf16[4,640,384]{2,1,0:T(8,128)(2,1)} %bitcast.19), calls=%async_computation | async-start | bytes 3932160 | tf_op jit(solution)/shard_map/all_to_all | solution.py:334
  7.8 12.8 %collective-permute-start = (bf16[192,256]{1,0:T(8,128)(2,1)S(1)}, bf16[192,256]{1,0:T(8,128)(2,1)S(1)}, u32[]{:S(2)}, u32[]{:S(2)}) collective-permute-start(bf16[192,256]{1,0:T(8,128)(2,1)S(1)} %copy-done), channel_id=1, source_target_pairs={{0,8},{4,12},{8,0},{12,4},{16,24},{20,28},{24,16},{28,20},{32,40},... | collective-permute-start | bytes 294920 | tf_op jit(solution)/shard_map/ppermute | solution.py:43
  9.5 13.6 %collective-permute-start.1 = (bf16[192,256]{1,0:T(8,128)(2,1)S(1)}, bf16[192,256]{1,0:T(8,128)(2,1)S(1)}, u32[]{:S(2)}, u32[]{:S(2)}) collective-permute-start(bf16[192,256]{1,0:T(8,128)(2,1)S(1)} %copy-done), channel_id=1, source_target_pairs={{0,64},{4,68},{8,72},{12,76},{16,80},{20,84},{24,88},{28,92},{32,9... | collective-permute-start | bytes 294920 | tf_op jit(solution)/shard_map/ppermute | solution.py:43
  10.7 12.4 %collective-permute-start.3 = (bf16[192,256]{1,0:T(8,128)(2,1)S(1)}, bf16[192,256]{1,0:T(8,128)(2,1)S(1)}, u32[]{:S(2)}, u32[]{:S(2)}) collective-permute-start(bf16[192,256]{1,0:T(8,128)(2,1)S(1)} %copy-done), channel_id=1, source_target_pairs={{0,128},{4,132},{8,136},{12,140},{16,144},{20,148},{24,152},{28,15... | collective-permute-start | bytes 294920 | tf_op jit(solution)/shard_map/ppermute | solution.py:43
  13.1 10.0 %collective-permute-start.5 = (bf16[192,256]{1,0:T(8,128)(2,1)S(1)}, bf16[192,256]{1,0:T(8,128)(2,1)S(1)}, u32[]{:S(2)}, u32[]{:S(2)}) collective-permute-start(bf16[192,256]{1,0:T(8,128)(2,1)S(1)} %copy-done), channel_id=1, source_target_pairs={{0,192},{4,196},{8,200},{12,204},{16,208},{20,212},{24,216},{28,22... | collective-permute-start | bytes 294920 | tf_op jit(solution)/shard_map/ppermute | solution.py:43
  13.3 12.1 %collective-permute-start.7 = (bf16[192,256]{1,0:T(8,128)(2,1)S(1)}, bf16[192,256]{1,0:T(8,128)(2,1)S(1)}, u32[]{:S(2)}, u32[]{:S(2)}) collective-permute-start(bf16[192,256]{1,0:T(8,128)(2,1)S(1)} %copy-done.1), channel_id=1, source_target_pairs={{0,160},{4,164},{8,168},{12,172},{16,176},{20,180},{24,184},{28,18... | collective-permute-start | bytes 294920 | tf_op jit(solution)/shard_map/ppermute | solution.py:47
  20.6 11.3 %collective-permute-start.8 = (bf16[192,256]{1,0:T(8,128)(2,1)S(1)}, bf16[192,256]{1,0:T(8,128)(2,1)S(1)}, u32[]{:S(2)}, u32[]{:S(2)}) collective-permute-start(bf16[192,256]{1,0:T(8,128)(2,1)S(1)} %copy-done.1), channel_id=1, source_target_pairs={{0,80},{4,84},{8,88},{12,92},{16,192},{20,196},{24,200},{28,204},{... | collective-permute-start | bytes 294920 | tf_op jit(solution)/shard_map/ppermute | solution.py:47
  23.0 9.4 %collective-permute-start.9 = (bf16[192,256]{1,0:T(8,128)(2,1)S(1)}, bf16[192,256]{1,0:T(8,128)(2,1)S(1)}, u32[]{:S(2)}, u32[]{:S(2)}) collective-permute-start(bf16[192,256]{1,0:T(8,128)(2,1)S(1)} %copy-done.1), channel_id=1, source_target_pairs={{0,240},{4,244},{8,248},{12,252},{16,96},{20,100},{24,104},{28,108... | collective-permute-start | bytes 294920 | tf_op jit(solution)/shard_map/ppermute | solution.py:47
  23.0 11.8 %collective-permute-start.2 = (bf16[192,256]{1,0:T(8,128)(2,1)S(1)}, bf16[192,256]{1,0:T(8,128)(2,1)S(1)}, u32[]{:S(2)}, u32[]{:S(2)}) collective-permute-start(bf16[192,256]{1,0:T(8,128)(2,1)S(1)} %collective-permute-done.refs_1_), channel_id=1, source_target_pairs={{0,64},{4,68},{8,72},{12,76},{16,80},{20,84},{24,88},{28,92},{32,9... | collective-permute-start | bytes 294920 | tf_op jit(solution)/shard_map/ppermute | solution.py:43
  23.1 11.7 %collective-permute-start.4 = (bf16[192,256]{1,0:T(8,128)(2,1)S(1)}, bf16[192,256]{1,0:T(8,128)(2,1)S(1)}, u32[]{:S(2)}, u32[]{:S(2)}) collective-permute-start(bf16[192,256]{1,0:T(8,128)(2,1)S(1)} %collective-permute-done.refs_1_), channel_id=1, source_target_pairs={{0,128},{4,132},{8,136},{12,140},{16,144},{20,148},{24,152},{28,15... | collective-permute-start | bytes 294920 | tf_op jit(solution)/shard_map/ppermute | solution.py:43
  25.5 9.8 %collective-permute-start.6 = (bf16[192,256]{1,0:T(8,128)(2,1)S(1)}, bf16[192,256]{1,0:T(8,128)(2,1)S(1)}, u32[]{:S(2)}, u32[]{:S(2)}) collective-permute-start(bf16[192,256]{1,0:T(8,128)(2,1)S(1)} %collective-permute-done.refs_1_), channel_id=1, source_target_pairs={{0,192},{4,196},{8,200},{12,204},{16,208},{20,212},{24,216},{28,22... | collective-permute-start | bytes 294920 | tf_op jit(solution)/shard_map/ppermute | solution.py:43
  31.9 3.4 %collective-permute-start.10 = (bf16[192,256]{1,0:T(8,128)(2,1)S(1)}, bf16[192,256]{1,0:T(8,128)(2,1)S(1)}, u32[]{:S(2)}, u32[]{:S(2)}) collective-permute-start(bf16[192,256]{1,0:T(8,128)(2,1)S(1)} %copy-done.1), channel_id=1, source_target_pairs={{0,4},{4,0},{8,12},{12,8},{16,20},{20,16},{24,28},{28,24},{32,36},... | collective-permute-start | bytes 294920 | tf_op jit(solution)/shard_map/ppermute | solution.py:51
  38.6 8.6 %collective-permute-start.14 = (bf16[2560,384]{1,0:T(8,128)(2,1)S(1)}, bf16[2560,384]{1,0:T(8,128)(2,1)S(1)}, u32[]{:S(2)}, u32[]{:S(2)}) collective-permute-start(bf16[2560,384]{1,0:T(8,128)(2,1)S(1)} %bitcast.14), channel_id=1, source_target_pairs={{0,4},{4,0},{8,12},{12,8},{16,20},{20,16},{24,28},{28,24},{32,36},... | collective-permute-start | bytes 5898248 | tf_op jit(solution)/shard_map/ppermute | solution.py:51
  51.4 5.3 %collective-permute-start.19 = (bf16[768,256]{1,0:T(8,128)(2,1)S(1)}, bf16[768,256]{1,0:T(8,128)(2,1)S(1)}, u32[]{:S(2)}, u32[]{:S(2)}) collective-permute-start(bf16[768,256]{1,0:T(8,128)(2,1)S(1)} %get-tuple-element.53), channel_id=1, source_target_pairs={{0,4},{4,0},{8,12},{12,8},{16,20},{20,16},{24,28},{28,24},{32,36},... | collective-permute-start | bytes 1179656 | tf_op jit(solution)/shard_map/ppermute | solution.py:51
  53.4 11.1 %collective-permute-start.15 = (bf16[384,128]{1,0:T(8,128)(2,1)S(1)}, bf16[384,128]{1,0:T(8,128)(2,1)S(1)}, u32[]{:S(2)}, u32[]{:S(2)}) collective-permute-start(bf16[384,128]{1,0:T(8,128)(2,1)S(1)} %get-tuple-element.49), channel_id=1, source_target_pairs={{0,128},{4,132},{8,136},{12,140},{16,144},{20,148},{24,152},{28,15... | collective-permute-start | bytes 294920 | tf_op jit(solution)/shard_map/ppermute | solution.py:43
  54.4 10.6 %collective-permute-start.16 = (bf16[384,128]{1,0:T(8,128)(2,1)S(1)}, bf16[384,128]{1,0:T(8,128)(2,1)S(1)}, u32[]{:S(2)}, u32[]{:S(2)}) collective-permute-start(bf16[384,128]{1,0:T(8,128)(2,1)S(1)} %get-tuple-element.50), channel_id=1, source_target_pairs={{0,64},{4,68},{8,72},{12,76},{16,80},{20,84},{24,88},{28,92},{32,9... | collective-permute-start | bytes 294920 | tf_op jit(solution)/shard_map/ppermute | solution.py:43
  54.8 10.1 %collective-permute-start.17 = (bf16[384,128]{1,0:T(8,128)(2,1)S(1)}, bf16[384,128]{1,0:T(8,128)(2,1)S(1)}, u32[]{:S(2)}, u32[]{:S(2)}) collective-permute-start(bf16[384,128]{1,0:T(8,128)(2,1)S(1)} %get-tuple-element.51), channel_id=1, source_target_pairs={{0,192},{4,196},{8,200},{12,204},{16,208},{20,212},{24,216},{28,22... | collective-permute-start | bytes 294920 | tf_op jit(solution)/shard_map/ppermute | solution.py:43
  56.8 9.9 %collective-permute-start.20 = (bf16[192,256]{1,0:T(8,128)(2,1)S(1)}, bf16[192,256]{1,0:T(8,128)(2,1)S(1)}, u32[]{:S(2)}, u32[]{:S(2)}) collective-permute-start(bf16[192,256]{1,0:T(8,128)(2,1)S(1)} %get-tuple-element.55), channel_id=1, source_target_pairs={{0,160},{4,164},{8,168},{12,172},{16,176},{20,180},{24,184},{28,18... | collective-permute-start | bytes 294920 | tf_op jit(solution)/shard_map/ppermute | solution.py:47
  63.1 10.1 %collective-permute-start.21 = (bf16[192,256]{1,0:T(8,128)(2,1)S(1)}, bf16[192,256]{1,0:T(8,128)(2,1)S(1)}, u32[]{:S(2)}, u32[]{:S(2)}) collective-permute-start(bf16[192,256]{1,0:T(8,128)(2,1)S(1)} %get-tuple-element.57), channel_id=1, source_target_pairs={{0,80},{4,84},{8,88},{12,92},{16,192},{20,196},{24,200},{28,204},{... | collective-permute-start | bytes 294920 | tf_op jit(solution)/shard_map/ppermute | solution.py:47
  64.5 9.1 %collective-permute-start.22 = (bf16[192,256]{1,0:T(8,128)(2,1)S(1)}, bf16[192,256]{1,0:T(8,128)(2,1)S(1)}, u32[]{:S(2)}, u32[]{:S(2)}) collective-permute-start(bf16[192,256]{1,0:T(8,128)(2,1)S(1)} %get-tuple-element.56), channel_id=1, source_target_pairs={{0,240},{4,244},{8,248},{12,252},{16,96},{20,100},{24,104},{28,108... | collective-permute-start | bytes 294920 | tf_op jit(solution)/shard_map/ppermute | solution.py:47
  65.0 8.8 %collective-permute-start.18 = (bf16[192,128]{1,0:T(8,128)(2,1)S(1)}, bf16[192,128]{1,0:T(8,128)(2,1)S(1)}, u32[]{:S(2)}, u32[]{:S(2)}) collective-permute-start(bf16[192,128]{1,0:T(8,128)(2,1)S(1)} %slice.98), channel_id=1, source_target_pairs={{0,8},{4,12},{8,0},{12,4},{16,24},{20,28},{24,16},{28,20},{32,40},... | collective-permute-start | bytes 147464 | tf_op jit(solution)/shard_map/ppermute | solution.py:43
  74.3 5.3 %collective-permute-start.23 = (bf16[192,384]{1,0:T(8,128)(2,1)S(1)}, bf16[192,384]{1,0:T(8,128)(2,1)S(1)}, u32[]{:S(2)}, u32[]{:S(2)}) collective-permute-start(bf16[192,384]{1,0:T(8,128)(2,1)S(1)} %pad_maximum_fusion), channel_id=1, source_target_pairs={{0,1},{1,2},{2,3},{3,0},{4,5},{5,6},{6,7},{7,4},{8,9},{9,10},{10,1... | collective-permute-start | bytes 442376 | tf_op jit(solution)/shard_map/ppermute | solution.py:321
  75.2 5.6 %collective-permute-start.25 = (bf16[192,384]{1,0:T(8,128)(2,1)S(1)}, bf16[192,384]{1,0:T(8,128)(2,1)S(1)}, u32[]{:S(2)}, u32[]{:S(2)}) collective-permute-start(bf16[192,384]{1,0:T(8,128)(2,1)S(1)} %pad_maximum_fusion), channel_id=1, source_target_pairs={{0,3},{1,0},{2,1},{3,2},{4,7},{5,4},{6,5},{7,6},{8,11},{9,8},{10,9... | collective-permute-start | bytes 442376 | tf_op jit(solution)/shard_map/ppermute | solution.py:321
  77.0 6.8 %collective-permute-start.24 = (bf16[192,384]{1,0:T(8,128)(2,1)S(1)}, bf16[192,384]{1,0:T(8,128)(2,1)S(1)}, u32[]{:S(2)}, u32[]{:S(2)}) collective-permute-start(bf16[192,384]{1,0:T(8,128)(2,1)S(1)} %pad_maximum_fusion), channel_id=1, source_target_pairs={{0,2},{1,3},{2,0},{3,1},{4,6},{5,7},{6,4},{7,5},{8,10},{9,11},{10,... | collective-permute-start | bytes 442376 | tf_op jit(solution)/shard_map/ppermute | solution.py:321
  (9 other events, 55.9 us)
